TPU v7x, 256 devices: a whole 4x4x8 slice. The times are simulated.
256 devices in a mesh: cfg: 2 (over x_lo), seq: 128 (over y, z, x_hi, core).
Axes of the slice: x: 4 (x_hi: 2, x_lo: 2; x = x_hi * 2 + x_lo), y: 4, z: 8, core: 2. Of those that a mesh axis runs over, the one named last changes fastest.
Arguments:
- coarse_hidden: bfloat16 [2, 256, 64, 2048], P('cfg', 'seq'), may hold values from -6 to 6
- coarse_modulation: float32 [2, 2, 2048], P('cfg'), may hold values from -3 to 3
- final_weight: bfloat16 [2048, 32], replicated, may hold values from -0.125 to 0.125
- coarse_latent: float32 [256, 2048], P('seq'), may hold values from -6 to 6
- step_index: int32 [1], replicated, may hold values from 0 to 49
- guide_index: int32 [1], replicated, may hold values from 0 to 4095
- guide_scales: float32 [4096], replicated, may hold values from 1.5 to 6
- upsample_weight: float32 [288, 32], replicated, may hold values from -0.375 to 0.375
- upsample_bias: float32 [32], replicated, may hold values from -3 to 3
- embed_weight: bfloat16 [32, 2048], replicated, may hold values from -1 to 1
- embed_bias: float32 [2048], replicated, may hold values from -3 to 3
- fine_modulation: float32 [3, 2048], replicated, may hold values from -3 to 3
- project_weight: bfloat16 [2048, 3072], P(('cfg', 'seq')), may hold values from -0.125 to 0.125
- query_gain: float32 [128], replicated, may hold values from 0.25 to 1.75
- key_gain: float32 [128], replicated, may hold values from 0.25 to 1.75
- text_keys: bfloat16 [256, 1024], replicated, may hold values from -6 to 6
- text_values: bfloat16 [256, 1024], replicated, may hold values from -6 to 6
- text_length: int32 [1], replicated, may hold values from 192 to 256
- output_weight: bfloat16 [1024, 2048], P(None, ('cfg', 'seq')), may hold values from -0.1875 to 0.1875
Outputs:
- guided_velocity: float32 [256, 2048], P('seq')
- fine_latent: float32 [256, 2, 4096], P('seq', 'cfg')
- fine_hidden: bfloat16 [256, 2, 128, 2048], P('seq', 'cfg')
All inputs are finite; a program needn't handle non-finite values.
Results may differ from a plain program's by a relative error of at most 0.0053.
Values may be sent and summed in bfloat16 or wider, within the bound.
A program may use at most 128 MiB of HBM per device.

v0:
```python
import jax
import jax.numpy as jnp
from jax import lax
from jax.sharding import PartitionSpec as P

HEADS = 8
STEPS = 50
epsilon = 1e-06
flow_shift = 5.0
highest = lax.Precision.HIGHEST


def from_partner(shard, axis, bit):
    return lax.ppermute(shard, axis, [(i, i ^ 1 << bit) for i in range(lax.axis_size(axis))])


def with_halo(block, sides, width):
    for axis, dim in sides:
        count = lax.axis_size(axis)
        forward = [(i, i + 1) for i in range(count - 1)]
        backward = [(target, source) for source, target in forward]
        low = lax.ppermute(
            lax.slice_in_dim(block, block.shape[dim] - width, None, axis=dim), axis, forward
        )
        high = lax.ppermute(lax.slice_in_dim(block, 0, width, axis=dim), axis, backward)
        block = jnp.concatenate([low, block, high], axis=dim)
    return block


def layer_norm(values):
    centred = values - jnp.mean(values, -1, keepdims=True)
    return centred * lax.rsqrt(jnp.mean(centred * centred, -1, keepdims=True) + epsilon)


def rms_heads(values, gain_vector, head_width):
    shaped = values.reshape(values.shape[0], -1, head_width)
    scaled = (
        shaped * lax.rsqrt(jnp.mean(shaped * shaped, -1, keepdims=True) + epsilon) * gain_vector
    )
    return scaled.reshape(values.shape[0], -1)


def sigma_at(step_value):
    fraction = 1.0 - step_value.astype(jnp.float32) / STEPS
    return flow_shift * fraction / (1.0 + (flow_shift - 1.0) * fraction)


def pick_scale(scale_table, slot_index):
    slots = jnp.arange(scale_table.shape[0], dtype=jnp.int32)
    return jnp.sum(jnp.where(slots == slot_index, scale_table, 0.0))


def attend(queries, image_keys, image_values, text_keys, text_values, image_mask, text_mask, heads):
    head_width = queries.shape[1] // heads
    score_scale = head_width ** (-0.5)
    dims = (((1,), (1,)), ((), ()))

    def one_head(head_index):
        column_start = head_index * head_width
        query_part = lax.dynamic_slice_in_dim(queries, column_start, head_width, 1)
        key_part = lax.dynamic_slice_in_dim(image_keys, column_start, head_width, 1)
        value_part = lax.dynamic_slice_in_dim(image_values, column_start, head_width, 1)
        text_key_part = lax.dynamic_slice_in_dim(text_keys, column_start, head_width, 1)
        text_value_part = lax.dynamic_slice_in_dim(text_values, column_start, head_width, 1)
        image_scores = (
            lax.dot_general(query_part, key_part, dims, preferred_element_type=jnp.float32)
            * score_scale
        )
        text_scores = (
            lax.dot_general(query_part, text_key_part, dims, preferred_element_type=jnp.float32)
            * score_scale
        )
        image_weights = jnp.where(image_mask, jnp.exp(image_scores), 0.0)
        text_weights = jnp.where(text_mask, jnp.exp(text_scores), 0.0)
        denominator = jnp.sum(image_weights, 1, keepdims=True) + jnp.sum(
            text_weights, 1, keepdims=True
        )
        image_weights = (image_weights / denominator).astype(jnp.bfloat16)
        text_weights = (text_weights / denominator).astype(jnp.bfloat16)
        return jnp.dot(image_weights, value_part, preferred_element_type=jnp.float32) + jnp.dot(
            text_weights, text_value_part, preferred_element_type=jnp.float32
        )

    stacked = lax.map(one_head, jnp.arange(heads, dtype=jnp.int32))
    return stacked.transpose(1, 0, 2).reshape(queries.shape[0], -1).astype(jnp.bfloat16)


def conv_rows(above, centre, below, upsample_weight, upsample_bias):
    tap_list = []
    for row_set in (above, centre, below):
        breadth = row_set.shape[1]
        padded = jnp.pad(row_set, ((0, 0), (1, 1), (0, 0)))
        for col_shift in range(3):
            tap_list.append(padded[:, col_shift : col_shift + breadth])
    patches = jnp.concatenate(tap_list, -1)
    flat_patches = patches.reshape(-1, patches.shape[-1])
    product = jnp.dot(flat_patches, upsample_weight, precision=highest).reshape(centre.shape)
    return product + upsample_bias + centre


def per_device(
    coarse_hidden,
    coarse_modulation,
    final_weight,
    coarse_latent,
    step_index,
    guide_index,
    guide_scales,
    upsample_weight,
    upsample_bias,
    embed_weight,
    embed_bias,
    fine_modulation,
    project_weight,
    query_gain,
    key_gain,
    text_keys,
    text_values,
    text_length,
    output_weight,
):
    row_count = coarse_hidden.shape[1]
    row_cells = coarse_hidden.shape[2]
    model_width = coarse_hidden.shape[3]
    channels = final_weight.shape[1]
    head_width = query_gain.shape[0]
    inner = project_weight.shape[1] // 3
    reach = max(row_count // 2, 1)
    branch = lax.axis_index("cfg")
    seq_index = lax.axis_index("seq")
    normed = layer_norm(coarse_hidden[0].astype(jnp.float32))
    modulated = (normed * (1.0 + coarse_modulation[0, 1]) + coarse_modulation[0, 0]).astype(
        jnp.bfloat16
    )
    velocity = jnp.dot(
        modulated.reshape(row_count * row_cells, model_width),
        final_weight,
        preferred_element_type=jnp.float32,
    ).reshape(row_count, row_cells * channels)
    partner = from_partner(velocity, "cfg", 0)
    conditional = jnp.where(branch == 0, velocity, partner)
    unconditional = jnp.where(branch == 0, partner, velocity)
    guidance = pick_scale(guide_scales, guide_index[0])
    guided = unconditional + guidance * (conditional - unconditional)
    stepped = coarse_latent + (sigma_at(step_index[0] + 1) - sigma_at(step_index[0])) * guided

    def embed_rows(grid_rows):
        grid_tokens = grid_rows.reshape(-1, channels).astype(jnp.bfloat16)
        state = jnp.dot(grid_tokens, embed_weight, preferred_element_type=jnp.float32) + embed_bias
        normed_state = (layer_norm(state) * (1.0 + fine_modulation[1]) + fine_modulation[0]).astype(
            jnp.bfloat16
        )
        return (state, normed_state)

    latent_grid = stepped.reshape(row_count, row_cells, channels)
    rim_width = reach + 1
    rimmed = with_halo(latent_grid, (("seq", 0),), rim_width)
    upsampled = jnp.repeat(jnp.repeat(rimmed, 2, 0), 2, 1)
    span = row_count + 2 * reach
    wide_grid = conv_rows(
        upsampled[1 : 1 + 2 * span],
        upsampled[2 : 2 + 2 * span],
        upsampled[3 : 3 + 2 * span],
        upsample_weight,
        upsample_bias,
    )
    grouped = wide_grid.reshape(span, 2, 2 * row_cells, channels)
    fine_grid = lax.dynamic_index_in_dim(
        grouped[reach : reach + row_count], branch, 1, keepdims=False
    )
    fine_state, fine_normed = embed_rows(fine_grid)

    def normed_rows(grid_rows):
        return embed_rows(grid_rows)[1]

    key_normed = lax.map(normed_rows, wide_grid.reshape(span, 4 * row_cells, channels)).reshape(
        -1, model_width
    )
    token_count = fine_normed.shape[0]
    weight_piece = lax.all_gather(project_weight, ("cfg", "seq"), axis=0, tiled=True)
    query_sum = jnp.dot(fine_normed, weight_piece[:, :inner], preferred_element_type=jnp.float32)
    key_sum = jnp.dot(
        key_normed, weight_piece[:, inner : 2 * inner], preferred_element_type=jnp.float32
    )
    value_sum = jnp.dot(
        key_normed, weight_piece[:, 2 * inner :], preferred_element_type=jnp.float32
    )
    queries = rms_heads(query_sum, query_gain, head_width).astype(jnp.bfloat16)
    keys = rms_heads(key_sum, key_gain, head_width).astype(jnp.bfloat16)
    values = value_sum.astype(jnp.bfloat16)
    image_keys, image_values = (keys, values)
    normed_text_keys = rms_heads(text_keys.astype(jnp.float32), key_gain, head_width).astype(
        jnp.bfloat16
    )
    key_count = image_keys.shape[0]
    query_rows = jnp.arange(token_count, dtype=jnp.int32) // (2 * row_cells)
    key_rows = jnp.arange(key_count, dtype=jnp.int32) // (4 * row_cells)
    distance = key_rows[None, :] - query_rows[:, None]
    global_rows = seq_index * row_count + key_rows - reach
    row_valid = (global_rows >= 0) & (global_rows < row_count * lax.axis_size("seq"))
    image_mask = (distance >= 0) & (distance <= 2 * reach) & row_valid[None, :]
    text_mask = (jnp.arange(text_keys.shape[0], dtype=jnp.int32) < text_length[0])[None, :]
    attended = attend(
        queries,
        image_keys,
        image_values,
        normed_text_keys,
        text_values,
        image_mask,
        text_mask,
        HEADS,
    )
    output_part = jnp.dot(
        attended,
        lax.all_gather(output_weight, ("cfg", "seq"), axis=1, tiled=True),
        preferred_element_type=jnp.float32,
    )
    fine_hidden = (fine_state + fine_modulation[2] * output_part).astype(jnp.bfloat16)
    fine_hidden = fine_hidden.reshape(row_count, 1, 2 * row_cells, model_width)
    fine_latent = fine_grid.reshape(row_count, 1, 2 * row_cells * channels)
    return (guided, fine_latent, fine_hidden)


def solution(mesh):
    placed = (
        P("cfg", "seq", None, None),
        P("cfg", None, None),
        P(),
        P("seq", None),
        P(),
        P(),
        P(),
        P(),
        P(),
        P(),
        P(),
        P(),
        P(("cfg", "seq"), None),
        P(),
        P(),
        P(),
        P(),
        P(),
        P(None, ("cfg", "seq")),
    )
    return jax.shard_map(
        per_device,
        mesh=mesh,
        in_specs=placed,
        out_specs=(P("seq", None), P("seq", "cfg", None), P("seq", "cfg", None, None)),
        check_vma=False,
    )
```

profile of v0, /device:TPU:32, one launch (start us, length us, event | category | flops | bytes accessed | tf_op | source)
XLA Modules:
  0.0 862.9 jit_solution(4221278181841568020)
XLA Ops:
  7.3 0.7 all-gather.3.cloned.1.call-update
  8.0 1.2 convert_reduce_fusion
  9.3 1.3 fusion.43
  10.7 0.8 slice_add_fusion.2
  11.5 1.4 fusion.47
  13.4 1.6 collective-permute-start
  17.6 1.1 fusion.39
  19.5 1.3 multiply_add_fusion
  20.9 1.9 collective-permute-start.1
  22.9 6.0 collective-permute-start.2
  29.0 1.8 collective-permute-done.2
  33.0 0.9 fusion.36
  34.1 9.6 %while.21 = (s32[]{:T(128)}, bf16[4,256,2048]{2,1,0:T(8,128)(2,1)}, bf16[4,256,32]{2,1,0:T(8,128)(2,1)S(1)}, bf16[32,2048]{1,0:T(8,128)(2,1)S(1)}, f32[2048]{0:T(1024)S(1)}, /*index=5*/f32[3,2048]{1,0:T(4,128)S(1)}, s32[]{:T(128)}) while((s32[]{:T(128)}, bf16[4,256,2048]{2,1,0:T(8,128)(2,1)}, bf16[4,256,32]{2,1,0:T(8,128)(2,1)S(1)}, ...), condition=%wide.region_9.10_spmd, body=%wide.region_6.9_spmd.sunk | while | flops 38799616 | bytes 7603793 | solution.py:176
  35.1 1.5 fusion.93
  37.5 1.5 fusion.93
  39.9 1.4 fusion.93
  42.2 1.4 fusion.93
  44.7 0.7 reshape.256
  45.5 392.8 %all-gather.3.cloned.1.call-done = bf16[2048,3072]{1,0:T(8,128)(2,1)} async-done(((bf16[8,3072]{1,0:T(8,128)(2,1)}), bf16[2048,3072]{1,0:T(8,128)(2,1)}) %all-gather.3.cloned.1.call-update) | async-done | bytes 12582928 | tf_op jit(solution)/shard_map/all_gather | solution.py:180
  438.2 4.6 slice_bitcast_fusion
  442.9 6.5 copy.109
  449.4 10.0 %multiply_reduce_fusion.1 = (f32[1024,8]{0,1:T(8,128)S(1)}, f32[1024,8,128]{0,2,1:T(8,128)}) fusion(bf16[1024,2048,1]{1,0,2:T(8,128)(2,1)} %bitcast.23, bf16[8,128,2048]{2,1,0:T(8,128)(2,1)} %bitcast.120), kind=kOutput, calls=%fused_computation.46 | convolution fusion | flops 4297056256 | bytes 12615680 | tf_op jit(solution)/shard_map/dot_general | solution.py:182
  459.4 3.5 fusion.29
  463.0 1.2 copy.136
  464.1 1.6 reduce_sum.113
  465.9 4.3 multiply_convert_fusion
  470.6 1.1 fusion.41
  471.7 9.4 %fusion.33 = bf16[1024,1024]{1,0:T(8,128)(2,1)} fusion(bf16[1024,2048]{1,0:T(8,128)(2,1)} %bitcast.22, bf16[2048,3072]{1,0:T(8,128)(2,1)} %all-gather.3.cloned.1.call-done), kind=kOutput, calls=%fused_computation.53 | convolution fusion | flops 4296015872 | bytes 10485760 | tf_op jit(solution)/shard_map/dot_general | solution.py:185
  481.0 57.2 %while.22 = (s32[]{:T(128)}, bf16[8,256,128]{1,2,0:T(8,128)(2,1)S(1)}, s32[8]{0:T(128)S(1)}, bf16[256,1024]{1,0:T(8,128)(2,1)}, bf16[1024,1024]{0,1:T(8,128)(2,1...) while((s32[]{:T(128)}, ...), condition=%wide.region_15.16_spmd.clone, body=%wide.region_12.15_spmd.clone.sunk | while | flops 170786816 | bytes 4013791 | solution.py:84
  482.2 1.6 fusion.97
  483.8 0.7 compare_reduce_fusion.2
  484.5 1.1 fusion.96
  485.6 1.1 fusion.98
  486.7 1.3 fusion.99
  489.4 1.6 fusion.97
  491.6 1.1 fusion.96
  492.8 1.1 fusion.98
  493.9 1.3 fusion.99
  496.5 1.6 fusion.97
  498.8 1.1 fusion.96
  499.9 1.1 fusion.98
  501.0 1.3 fusion.99
  503.6 1.6 fusion.97
  505.9 1.1 fusion.96
  507.0 1.1 fusion.98
  508.1 1.3 fusion.99
  510.8 1.6 fusion.97
  513.1 1.1 fusion.96
  514.2 1.1 fusion.98
  515.3 1.3 fusion.99
  517.9 1.6 fusion.97
  520.2 1.1 fusion.96
  521.3 1.1 fusion.98
  522.4 1.3 fusion.99
  525.1 1.6 fusion.97
  527.4 1.1 fusion.96
  528.5 1.1 fusion.98
  529.6 1.3 fusion.99
  532.2 1.6 fusion.97
  534.5 1.1 fusion.96
  535.6 1.1 fusion.98
  536.7 1.3 fusion.99
  538.2 313.4 %all-gather.5.cloned.1.call-done = bf16[1024,2048]{0,1:T(8,128)(2,1)} async-done(((bf16[1024,8]{0,1:T(8,128)(2,1)}), bf16[1024,2048]{0,1:T(8,128)(2,1)}) %all-gather.5.cloned.1.call-update) | async-done | bytes 4194320 | tf_op jit(solution)/shard_map/all_gather | solution.py:215
  851.6 4.5 fusion.32
  (153 shorter events, 20.5 us)
Async XLA Ops:
  7.2 5.8 copy-start
  7.2 8.4 copy-start.3
  7.2 8.5 copy-start.10
  7.2 8.5 copy-start.2
  7.2 431.0 %all-gather.3.cloned.1.call-start = ((), (), s32[]{:S(2)}) async-start(), calls=%async_computation | async-start | bytes 12632064 | tf_op jit(solution)/shard_map/all_gather | solution.py:180
  7.9 843.7 %all-gather.5.cloned.1.call-start = ((), (), s32[]{:S(2)}) async-start(), calls=%async_computation.1 | async-start | bytes 4210688 | tf_op jit(solution)/shard_map/all_gather | solution.py:215
  13.4 6.1 collective-permute-start
  15.8 0.8 copy-start.8
  15.8 0.8 copy-start.6
  16.4 3.1 copy-start.7
  20.9 8.1 collective-permute-start.1
  22.9 7.9 collective-permute-start.2
  31.8 1.1 copy-start.5
  31.9 1.1 copy-start.9
  32.5 1.6 copy-start.1
  32.5 1.6 copy-start.4
  471.7 9.4 %copy-start.11 = (bf16[8,256,128]{1,2,0:T(8,128)(2,1)S(1)}, bf16[8,256,128]{1,2,0:T(8,128)(2,1)}, u32[]{:S(2)}) copy-start(bf16[8,256,128]{1,2,0:T(8,128)(2,1)} %custom-call.3) | copy-start | bytes 1572868
Sparse Core Ops, SparseCore 0:
  9.9 428.2 all-gather.2
  440.1 411.4 all-gather.4
where the time goes:
time: 865 us; the launch traced here: 863 us
  waiting for transfers between devices  709 us (82%)
  matrix products  71.9 us (8%)
  other arithmetic  28.6 us (3%)
  local copies, waits for them, and re-layouts  22.7 us (3%)
  between operations  16 us (2%)
  starting transfers between devices  9.62 us (1%)
    all_gather x1, waiting for transfers between devices, per_device(): lax.all_gather(project_weight, ('cfg', 'seq'), axis=0, tiled=True)  393 us
    all_gather x1, waiting for transfers between devices, per_device(): lax.all_gather(output_weight, ('cfg', 'seq'), axis=1, tiled=True)  313 us
  transfers between devices with their start and end apart: 5, of which 4 were waited for; matrix products, arithmetic and copies ran while one was open for 14% of the time, Pallas kernels for 0%

commit v1 on v0

--- a/solution.py
+++ b/solution.py
@@ -177,7 +177,12 @@
         -1, model_width
     )
     token_count = fine_normed.shape[0]
-    weight_piece = lax.all_gather(project_weight, ("cfg", "seq"), axis=0, tiled=True)
+    weight_piece = jnp.concatenate(
+        lax.all_to_all(
+            jnp.stack([project_weight] * lax.axis_size(("cfg", "seq"))), ("cfg", "seq"), 0, 0
+        ),
+        axis=0,
+    )
     query_sum = jnp.dot(fine_normed, weight_piece[:, :inner], preferred_element_type=jnp.float32)
     key_sum = jnp.dot(
         key_normed, weight_piece[:, inner : 2 * inner], preferred_element_type=jnp.float32

time: 865 us -> 548 us (0.63)
  the two profiles are of different devices: /device:TPU:32 before, /device:TPU:100 now
where the time goes in v1:
time: 548 us; the launch traced here: 546 us
  waiting for transfers between devices  380 us (69%)
  matrix products  68.3 us (12%)
  local copies, waits for them, and re-layouts  30.1 us (5%)
  starting transfers between devices  23.2 us (4%)
  other arithmetic  22.5 us (4%)
  between operations  16 us (3%)
  loops' own time  6.29 us (1%)
    all_to_all x1, waiting for transfers between devices, per_device(): lax.all_to_all(jnp.stack([project_weight] * lax.axis_size(('cfg', 'seq'))...  223 us
    all_gather x1, waiting for transfers between devices, per_device(): lax.all_gather(output_weight, ('cfg', 'seq'), axis=1, tiled=True)  127 us
    ppermute x1, waiting for transfers between devices, from_partner(): lax.ppermute(shard, axis, [(i, i ^ 1 << bit) for i in range(lax.axis_size...  27.2 us
    all_to_all x1, starting transfers between devices, per_device(): lax.all_to_all(jnp.stack([project_weight] * lax.axis_size(('cfg', 'seq'))...  14.9 us
    dot_general x8, matrix products, one_head(): lax.dot_general(query_part, key_part, dims, preferred_element_type=jnp.fl...  13 us
    dot_general x2, local copies, waits for them, and re-layouts, per_device(): jnp.dot(key_normed, weight_piece[:, inner:2 * inner], preferred_element_t...  11.1 us
  transfers between devices with their start and end apart: 5, of which 5 were waited for; matrix products, arithmetic and copies ran while one was open for 20% of the time, Pallas kernels for 0%

profile of v1, /device:TPU:100, one launch (start us, length us, event | category | flops | bytes accessed | tf_op | source)
XLA Modules:
  0.0 546.3 jit_solution(17606746739691629248)
XLA Ops:
  7.2 6.9 %stack.2 = bf16[256,8,3072]{2,1,0:T(8,128)(2,1)} broadcast(bf16[8,3072]{1,0:T(8,128)(2,1)} %param.35), dimensions={1,2} | broadcast | bytes 12632064 | tf_op jit(solution)/shard_map/stack | solution.py:182
  14.1 14.9 %all-to-all-start = ((bf16[256,8,3072]{2,1,0:T(8,128)(2,1)}), bf16[256,8,3072]{2,1,0:T(8,128)(2,1)}, u32[]{:S(2)}, u32[]{:S(2)}) async-start(bf16[256,8,3072]{2,1,0:T(8,128)(2,1)} %stack.2), calls=%async_computation | async-start | bytes 25165824 | tf_op jit(solution)/shard_map/all_to_all | solution.py:181
  30.5 1.3 collective-permute-start
  34.4 1.1 fusion.39
  36.3 27.2 %collective-permute-done = f32[2,2048]{1,0:T(2,128)S(1)} collective-permute-done((f32[2,2048]{1,0:T(2,128)S(1)}, f32[2,2048]{1,0:T(2,128)S(1)}, u32[]{:S(2)}, u32[]{:S(2)}) %collective-permute-start) | collective-permute-done | bytes 16416 | tf_op jit(solution)/shard_map/ppermute | solution.py:14
  63.5 1.3 multiply_add_fusion
  64.8 1.9 collective-permute-start.1
  66.8 5.1 collective-permute-start.2
  72.0 2.0 collective-permute-done.1
  76.2 0.9 fusion.36
  77.4 0.7 reshape.262
  79.1 9.6 %while.21 = (s32[]{:T(128)}, bf16[4,256,2048]{2,1,0:T(8,128)(2,1)}, bf16[4,256,32]{2,1,0:T(8,128)(2,1)S(1)}, bf16[32,2048]{1,0:T(8,128)(2,1)S(1)}, f32[2048]{0:T(1024)S(1)}, /*index=5*/f32[3,2048]{1,0:T(4,128)S(1)}, s32[]{:T(128)}) while((s32[]{:T(128)}, bf16[4,256,2048]{2,1,0:T(8,128)(2,1)}, bf16[4,256,32]{2,1,0:T(8,128)(2,1)S(1)}, ...), condition=%wide.region_9.10_spmd, body=%wide.region_6.9_spmd.sunk | while | flops 38799616 | bytes 7603293 | solution.py:176
  80.2 1.5 fusion.93
  82.6 1.4 fusion.93
  84.9 1.4 fusion.93
  87.2 1.5 fusion.93
  88.7 223.2 %all-to-all-done = bf16[256,8,3072]{2,1,0:T(8,128)(2,1)} async-done(((bf16[256,8,3072]{2,1,0:T(8,128)(2,1)}), bf16[256,8,3072]{2,1,0:T(8,128)(2,1)}, u32[]{:S(2)}, u32[]{:S(2)}) %all-to-all-start) | async-done | bytes 12582944 | tf_op jit(solution)/shard_map/all_to_all | solution.py:181
  311.9 4.6 slice_bitcast_fusion
  316.5 3.5 fusion.29
  320.1 1.2 copy.136
  321.2 1.6 reduce_sum.113
  323.0 6.5 %copy.109 = bf16[1024,2048]{1,0:T(8,128)(2,1)} copy(bf16[1024,2048]{0,1:T(8,128)(2,1)} %slice_bitcast_fusion) | data formatting | bytes 8388608 | tf_op jit(solution)/shard_map/dot_general | solution.py:187
  329.5 7.8 %multiply_reduce_fusion.1 = (f32[1024,8]{0,1:T(8,128)S(1)}, f32[1024,8,128]{0,2,1:T(8,128)S(1)}) fusion(bf16[1024,2048,1]{1,0,2:T(8,128)(2,1)} %bitcast.141, bf16[8,128,2048]{2,1,0:T(8,128)(2,1)} %bitcast.121), kind=kOutput, calls=%fused_computation.46 | convolution fusion | flops 4297056256 | bytes 12615680 | tf_op jit(solution)/shard_map/dot_general | solution.py:187
  337.4 7.9 %fusion.33 = bf16[1024,1024]{1,0:T(8,128)(2,1)} fusion(bf16[1024,2048]{1,0:T(8,128)(2,1)S(1)} %bitcast.142, bf16[2048,3072]{1,0:T(8,128)(2,1)} %bitcast.20), kind=kOutput, calls=%fused_computation.53 | convolution fusion | flops 4296015872 | bytes 10485760 | tf_op jit(solution)/shard_map/dot_general | solution.py:190
  345.6 1.1 fusion.41
  346.7 2.2 multiply_convert_fusion
  348.9 58.7 %while.22 = (s32[]{:T(128)}, bf16[8,256,128]{1,2,0:T(8,128)(2,1)S(1)}, s32[8]{0:T(128)S(1)}, bf16[256,1024]{1,0:T(8,128)(2,1)}, bf16[1024,1024]{0,1:T(8,128)(2,1...) while((s32[]{:T(128)}, ...), condition=%wide.region_15.16_spmd.clone, body=%wide.region_12.15_spmd.clone.sunk | while | flops 170786816 | bytes 4013799 | solution.py:84
  350.9 1.1 fusion.96
  352.0 1.6 fusion.97
  353.6 1.1 fusion.98
  354.7 1.3 fusion.99
  357.6 0.7 compare_reduce_fusion.2
  358.2 1.1 fusion.96
  359.4 1.6 fusion.97
  361.0 1.1 fusion.98
  362.1 1.3 fusion.99
  364.9 0.7 compare_reduce_fusion.2
  365.6 1.1 fusion.96
  366.7 1.6 fusion.97
  368.3 1.1 fusion.98
  369.4 1.3 fusion.99
  372.3 0.7 compare_reduce_fusion.2
  372.9 1.1 fusion.96
  374.0 1.6 fusion.97
  375.7 1.1 fusion.98
  376.7 1.3 fusion.99
  380.3 1.1 fusion.96
  381.4 1.6 fusion.97
  383.0 1.1 fusion.98
  384.1 1.3 fusion.99
  387.6 1.1 fusion.96
  388.7 1.6 fusion.97
  390.3 1.1 fusion.98
  391.4 1.3 fusion.99
  394.9 1.1 fusion.96
  396.0 1.6 fusion.97
  397.7 1.1 fusion.98
  398.8 1.3 fusion.99
  402.3 1.1 fusion.96
  403.4 1.6 fusion.97
  405.0 1.1 fusion.98
  406.1 1.3 fusion.99
  407.6 127.4 %all-gather.2.cloned.1.call-done = bf16[1024,2048]{0,1:T(8,128)(2,1)} async-done(((bf16[1024,8]{0,1:T(8,128)(2,1)}), bf16[1024,2048]{0,1:T(8,128)(2,1)}) %all-gather.2.cloned.1.call-update) | async-done | bytes 4194320 | tf_op jit(solution)/shard_map/all_gather | solution.py:220
  535.0 4.5 fusion.32
  (161 shorter events, 20.5 us)
Async XLA Ops:
  7.2 22.9 %copy-start = (bf16[2048,32]{0,1:T(8,128)(2,1)S(1)}, bf16[2048,32]{0,1:T(8,128)(2,1)}, u32[]{:S(2)}) copy-start(bf16[2048,32]{0,1:T(8,128)(2,1)} %param.25) | copy-start | bytes 393220
  14.1 14.9 %copy-start.3 = (bf16[1,2,64,2048]{3,2,1,0:T(8,128)(2,1)S(1)}, bf16[1,2,64,2048]{3,2,1,0:T(8,128)(2,1)}, u32[]{:S(2)}) copy-start(bf16[1,2,64,2048]{3,2,1,0:T(8,128)(2,1)} %param.23) | copy-start | bytes 1572868
  14.1 15.6 %copy-start.8 = (f32[1,2,2048]{2,1,0:T(2,128)S(1)}, f32[1,2,2048]{2,1,0:T(2,128)}, u32[]{:S(2)}) copy-start(f32[1,2,2048]{2,1,0:T(2,128)} %param.24) | copy-start | bytes 49156
  14.1 297.8 %all-to-all-start = ((bf16[256,8,3072]{2,1,0:T(8,128)(2,1)}), bf16[256,8,3072]{2,1,0:T(8,128)(2,1)}, u32[]{:S(2)}, u32[]{:S(2)}) async-start(bf16[256,8,3072]{2,1,0:T(8,128)(2,1)} %stack.2), calls=%async_computation | async-start | bytes 25165824 | tf_op jit(solution)/shard_map/all_to_all | solution.py:181
  29.0 3.5 copy-start.4
  29.0 506.0 %all-gather.2.cloned.1.call-start = ((), (), s32[]{:S(2)}) async-start(), calls=%async_computation.1 | async-start | bytes 4210688 | tf_op jit(solution)/shard_map/all_gather | solution.py:220
  30.5 33.0 %collective-permute-start = (f32[2,2048]{1,0:T(2,128)S(1)}, f32[2,2048]{1,0:T(2,128)S(1)}, u32[]{:S(2)}, u32[]{:S(2)}) collective-permute-start(f32[2,2048]{1,0:T(2,128)S(1)} %reshape.240), channel_id=1, source_target_pairs={{0,128},{128,0},{1,129},{129,1},{2,130},{130,2},{3,131},{131,3},{4... | collective-permute-start | bytes 49160 | tf_op jit(solution)/shard_map/ppermute | solution.py:14
  32.6 0.8 copy-start.9
  32.6 1.4 copy-start.13
  32.6 1.4 copy-start.11
  33.2 2.3 copy-start.5
  33.2 30.3 %copy-start.10 = (f32[2,2048]{1,0:T(2,128)S(1)}, f32[2,2048]{1,0:T(2,128)}, u32[]{:S(2)}) copy-start(f32[2,2048]{1,0:T(2,128)} %param.26) | copy-start | bytes 49156
  64.8 9.1 %collective-permute-start.1 = (f32[2,64,32]{2,1,0:T(8,128)S(1)}, f32[2,64,32]{2,1,0:T(8,128)S(1)}, u32[]{:S(2)}, u32[]{:S(2)}) collective-permute-start(f32[2,64,32]{2,1,0:T(8,128)S(1)} %reshape.241), channel_id=1, source_target_pairs={{0,1},{1,2},{2,3},{3,4},{4,5},{5,6},{6,7},{7,8},{8,9},{9,10},{10,1... | collective-permute-start | bytes 49160 | tf_op jit(solution)/shard_map/ppermute | solution.py:22
  66.8 7.2 %collective-permute-start.2 = (f32[2,64,32]{2,1,0:T(8,128)S(1)}, f32[2,64,32]{2,1,0:T(8,128)S(1)}, u32[]{:S(2)}, u32[]{:S(2)}) collective-permute-start(f32[2,64,32]{2,1,0:T(8,128)S(1)} %reshape.241), channel_id=1, source_target_pairs={{1,0},{2,1},{3,2},{4,3},{5,4},{6,5},{7,6},{8,7},{9,8},{10,9},{11,1... | collective-permute-start | bytes 49160 | tf_op jit(solution)/shard_map/ppermute | solution.py:25
  75.0 1.1 copy-start.7
  75.0 1.1 copy-start.12
  75.6 2.5 copy-start.2
  75.6 2.5 copy-start.6
  329.5 7.8 %copy-start.14 = (bf16[4,256,2048]{2,1,0:T(8,128)(2,1)S(1)}, bf16[4,256,2048]{2,1,0:T(8,128)(2,1)}, u32[]{:S(2)}) copy-start(bf16[4,256,2048]{2,1,0:T(8,128)(2,1)} %get-tuple-element.87) | copy-start | bytes 12582916
  346.7 2.2 copy-start.15
  535.0 4.5 copy-start.1
Sparse Core Ops, SparseCore 0:
  31.9 502.9 all-gather.1
